TPU v7x, 128 devices: a whole 4x4x4 slice. The times are simulated.
128 devices in a mesh: group: 8 (over y, core), dp: 16 (over x, z).
Axes of the slice: x: 4, y: 4, z: 4, core: 2. Of those that a mesh axis runs over, the one named last changes fastest.
Arguments:
- acts: bfloat16 [131072, 2048], P(('group', 'dp')), may hold values from -6 to 6
- grad_out: bfloat16 [131072, 2048], P(('group', 'dp')), may hold values from -0.1875 to 0.1875
- error_in: bfloat16 [262144, 2048], P(('group', 'dp')), may hold values from -6 to 6
- kept: int32 [128, 328], P(('group', 'dp')), may hold values from 0 to 32767, as said below
- bounds: int32 [17], replicated, may hold values from 0 to 32768, as said below
Outputs:
- new_error: bfloat16 [262144, 2048], P(('group', 'dp'))
- regathered: float32 [128, 328, 128], P(('group', 'dp'))
Inputs may be any that keep to these rules, and one draw needn't show every extreme that they name: `kept`: row d lists 328 different block numbers in no particular order. In each group one region (drawn per group) holds exactly 80 of every device's blocks; each device's other blocks lie in the other regions with counts that differ by at most one. bounds[0] = 0 and bounds[16] = 32768; every region holds at least 1024 blocks and at most 3072, and some region exactly 3072.
All inputs are finite; a program needn't handle non-finite values.
Results may differ from a plain program's by a relative error of at most 0.001.
Values sent between devices are 32-bit elements; how exact they have to be, the bound alone decides.
A program may use at most 128 MiB of HBM per device.

v0:
```python
import jax
import jax.numpy as jnp
from jax import lax
from jax.sharding import PartitionSpec as P

CAP = 80


def regather(values, ids, bounds, owners, owner_index, regmax):
    limits = bounds[1:owners]
    owner = jnp.sum((ids[:, None] >= limits[None, :]).astype(jnp.int32), axis=1)
    onehot = (owner[:, None] == jnp.arange(owners, dtype=jnp.int32)[None, :]).astype(jnp.int32)
    before = jnp.cumsum(onehot, axis=0) - onehot
    slot = jnp.sum(before * onehot, axis=1)
    position = owner * CAP + slot
    send_vals = (
        jnp.zeros((owners * CAP, 128), jnp.float32)
        .at[position]
        .set(values)
        .reshape(owners, CAP, 128)
    )
    send_ids = jnp.full((owners * CAP,), -1, jnp.int32).at[position].set(ids).reshape(owners, CAP)
    got_vals, got_ids = (
        lax.all_to_all(send_vals, "dp", split_axis=0, concat_axis=0, tiled=True),
        lax.all_to_all(send_ids, "dp", split_axis=0, concat_axis=0, tiled=True),
    )
    first = bounds[owner_index]
    local = jnp.where(got_ids >= 0, got_ids - first, regmax).reshape(-1)
    flat_vals = got_vals.reshape(-1, 128)
    empty = jnp.zeros((regmax, 128), jnp.float32)
    region = lax.psum(empty.at[local].add(flat_vals, mode="drop"), "group")
    extent = (bounds[owner_index + 1] - first).astype(jnp.float32)
    region_rms = jnp.sqrt(jnp.sum(region * region) / (extent * 128.0) + 1e-06)
    answer = region.at[local].get(mode="fill", fill_value=0.0) / region_rms
    back = lax.all_to_all(
        answer.reshape(owners, CAP, 128), "dp", split_axis=0, concat_axis=0, tiled=True
    )
    return back.reshape(owners * CAP, 128)[position]


def body(acts, grad_out, error_in, kept, bounds):
    width = acts.shape[1]
    per_row = width // 128
    nblocks = width * per_row
    owners = lax.axis_size("dp")
    owner_index = lax.axis_index("dp")
    base = nblocks // owners
    regmax = base + 2 * (base // 4)
    ids = kept[0]
    full = jnp.einsum(
        "td,te->de", acts, grad_out, preferred_element_type=jnp.float32
    ) + error_in.astype(jnp.float32)
    blocks = full.reshape(nblocks, 128)
    values = blocks[ids]
    result = regather(values, ids, bounds, owners, owner_index, regmax)
    new_error = blocks.at[ids].set(0.0).reshape(width, width).astype(jnp.bfloat16)
    return (new_error, result[None])


def solution(mesh):
    in_specs = (
        P(("group", "dp"), None),
        P(("group", "dp"), None),
        P(("group", "dp"), None),
        P(("group", "dp"), None),
        P(),
    )
    out_specs = (P(("group", "dp"), None), P(("group", "dp"), None, None))
    return jax.shard_map(body, mesh=mesh, in_specs=in_specs, out_specs=out_specs, check_vma=False)
```

profile of v0, /device:TPU:1, one launch (start us, length us, event | category | flops | bytes accessed | tf_op | source)
XLA Modules:
  0.0 208.5 jit_solution(6665105610771437842)
XLA Ops:
  7.2 0.7 slice.12
  7.9 0.7 reduce.1
  8.6 0.1 convert_reduce_fusion
  8.7 0.9 reduce-window.6
  9.6 0.2 slice_reduce_fusion
  9.8 0.1 bitcast_bitcast_fusion
  10.0 2.9 %scatter_custom_fusion.1 = s32[1280]{0:T(1024)S(1)} fusion(s32[328]{0:T(512)S(1)} %fusion.13, s32[328]{0:T(512)S(1)} %reduce.1, s32[]{:T(128)} %constant.18.clone.1), kind=kCustom, calls=%fused_computation.38 | custom fusion | bytes 5124 | tf_op jit(solution)/shard_map/scatter | solution.py:22
  12.9 0.7 all_to_all.12
  13.6 8.4 %all-to-all-start = ((s32[16,1,80]{2,1,0:T(1,128)}), s32[16,1,80]{2,1,0:T(1,128)S(1)}, u32[]{:S(2)}, u32[]{:S(2)}) async-start(s32[16,1,80]{2,1,0:T(1,128)} %all_to_all.12), calls=%async_computation | async-start | bytes 16384 | tf_op jit(solution)/shard_map/all_to_all | solution.py:25
  22.0 0.7 fusion.12
  22.7 16.5 %convert_add_fusion = f32[2048,2048]{1,0:T(8,128)} fusion(bf16[2048,2048]{1,0:T(8,128)(2,1)} %param.7, bf16[1024,2048]{1,0:T(8,128)(2,1)} %param.5, bf16[1024,2048]{1,0:T(8,128)(2,1)} %param.6), kind=kOutput, calls=%fused_computation.7 | convolution fusion | flops 8598323200 | bytes 33554432 | tf_op jit(solution)/shard_map/td,te->de/dot_general | solution.py:50
  39.2 0.0 copy-start.1
  39.2 18.0 %reshape.148 = f32[32768,128]{1,0:T(8,128)} reshape(f32[2048,2048]{1,0:T(8,128)} %convert_add_fusion) | data formatting | bytes 33554432 | tf_op jit(solution)/shard_map/reshape | solution.py:53
  57.2 4.3 %scatter_custom_fusion.2 = f32[1280,128]{1,0:T(8,128)} fusion(s32[328]{0:T(512)S(1)} %fusion.13, f32[]{:T(128)} %constant.17.clone.1, f32[32768,128]{1,0:T(8,128)} %reshape.148, s32[1024]{0:T(1024)S(1)} %pad_clamp_fusion.2), kind=kCustom, calls=%fused_computation.12 | custom fusion | bytes 655872 | tf_op jit(solution)/shard_map/scatter | solution.py:19
  61.5 0.0 all-to-all-done
  61.5 6.7 %all-to-all-start.1 = ((f32[16,80,128]{2,1,0:T(8,128)}), f32[16,80,128]{2,1,0:T(8,128)S(1)}, u32[]{:S(2)}, u32[]{:S(2)}) async-start(f32[16,80,128]{2,1,0:T(8,128)} %bitcast.4), calls=%async_computation.1 | async-start | bytes 1310720 | tf_op jit(solution)/shard_map/all_to_all | solution.py:24
  68.1 0.0 all-reduce.3.cloned.1.call-start
  68.2 0.0 copy-done.1
  68.2 0.7 fusion.15
  68.9 0.5 broadcast.182
  69.4 1.3 fusion.14
  70.7 0.1 select_n.76
  70.8 8.9 %all-to-all-done.1 = f32[16,80,128]{2,1,0:T(8,128)S(1)} async-done(((f32[16,80,128]{2,1,0:T(8,128)}), f32[16,80,128]{2,1,0:T(8,128)S(1)}, u32[]{:S(2)}, u32[]{:S(2)}) %all-to-all-start.1) | async-done | bytes 655392 | tf_op jit(solution)/shard_map/all_to_all | solution.py:24
  79.7 10.1 %scatter_custom_fusion.3 = f32[3072,128]{1,0:T(8,128)} fusion(s32[1280]{0:T(1024)S(1)} %fusion.9, f32[1280,128]{1,0:T(8,128)S(1)} %bitcast.27, f32[]{:T(128)} %constant.17.clone.1), kind=kCustom, calls=%fused_computation.9 | custom fusion | flops 163840 | bytes 1572868 | tf_op jit(solution)/shard_map/scatter-add | solution.py:31
  89.8 0.0 all-reduce.3.cloned.1.call-update
  91.1 60.6 %all-reduce.3.cloned.1.call-done = f32[3072,128]{1,0:T(8,128)} async-done(((f32[3072,128]{1,0:T(8,128)}), f32[3072,128]{1,0:T(8,128)}) %all-reduce.3.cloned.1.call-update) | async-done | bytes 1572880 | tf_op jit(solution)/shard_map/psum | solution.py:31
  151.7 0.0 copy-start
  151.7 2.5 %multiply_reduce_fusion = f32[]{:T(128)} fusion(f32[3072,128]{1,0:T(8,128)} %all-reduce.3.cloned.1.call-done), kind=kLoop, calls=%fused_computation.8 | loop fusion | flops 786431 | bytes 1572868 | tf_op jit(solution)/shard_map/reduce_sum | solution.py:33
  154.9 0.0 copy-done
  154.9 2.4 %gather_fusion = f32[1280,128]{1,0:T(8,128)S(1)} fusion(f32[3072,128]{1,0:T(8,128)S(1)} %copy-done, s32[2048]{0:T(1024)S(1)} %pad_clamp_fusion), kind=kCustom, calls=%fused_computation.1 | custom fusion | bytes 1315840 | tf_op jit(solution)/shard_map/gather | solution.py:34
  157.3 1.1 select_divide_fusion
  158.4 6.7 %all-to-all-start.2 = ((f32[16,80,128]{2,1,0:T(8,128)}), f32[16,80,128]{2,1,0:T(8,128)S(1)}, u32[]{:S(2)}, u32[]{:S(2)}) async-start(f32[16,80,128]{2,1,0:T(8,128)} %select_divide_fusion), calls=%async_computation.2 | async-start | bytes 1310720 | tf_op jit(solution)/shard_map/all_to_all | solution.py:35
  165.1 12.8 %scatter_custom_fusion = f32[32768,128]{1,0:T(8,128)} fusion(f32[32768,128]{1,0:T(8,128)} %reshape.148, s32[328]{0:T(512)S(1)} %fusion.12, f32[]{:T(128)} %constant.17.clone.1), kind=kCustom, calls=%fused_computation.15 | custom fusion | bytes 16777728 | tf_op jit(solution)/shard_map/scatter | solution.py:56
  177.8 8.9 %convert_element_type.20 = bf16[32768,128]{1,0:T(8,128)(2,1)} convert(f32[32768,128]{1,0:T(8,128)} %scatter_custom_fusion) | non-fusion elementwise | flops 4194304 | bytes 25165824 | tf_op jit(solution)/shard_map/convert_element_type | solution.py:56
  186.7 13.3 %convert_element_type.21 = bf16[2048,2048]{1,0:T(8,128)(2,1)} reshape(bf16[32768,128]{1,0:T(8,128)(2,1)} %convert_element_type.20) | data formatting | bytes 16777216 | tf_op jit(solution)/shard_map/convert_element_type | solution.py:56
  200.0 0.0 all-to-all-done.2
  200.0 1.6 gather_fusion.1
  (11 shorter events, 0.2 us)
Async XLA Ops:
  13.6 47.9 %all-to-all-start = ((s32[16,1,80]{2,1,0:T(1,128)}), s32[16,1,80]{2,1,0:T(1,128)S(1)}, u32[]{:S(2)}, u32[]{:S(2)}) async-start(s32[16,1,80]{2,1,0:T(1,128)} %all_to_all.12), calls=%async_computation | async-start | bytes 16384 | tf_op jit(solution)/shard_map/all_to_all | solution.py:25
  39.2 29.0 %copy-start.1 = (s32[17]{0:T(128)S(1)}, s32[17]{0:T(128)}, u32[]{:S(2)}) copy-start(s32[17]{0:T(128)} %param.9) | copy-start | bytes 208
  61.5 18.2 %all-to-all-start.1 = ((f32[16,80,128]{2,1,0:T(8,128)}), f32[16,80,128]{2,1,0:T(8,128)S(1)}, u32[]{:S(2)}, u32[]{:S(2)}) async-start(f32[16,80,128]{2,1,0:T(8,128)} %bitcast.4), calls=%async_computation.1 | async-start | bytes 1310720 | tf_op jit(solution)/shard_map/all_to_all | solution.py:24
  68.1 83.5 %all-reduce.3.cloned.1.call-start = ((), (), s32[]{:S(2)}) async-start(), calls=%async_computation.3 | async-start | bytes 3145728 | tf_op jit(solution)/shard_map/psum | solution.py:31
  151.7 3.2 %copy-start = (f32[3072,128]{1,0:T(8,128)S(1)}, f32[3072,128]{1,0:T(8,128)}, u32[]{:S(2)}) copy-start(f32[3072,128]{1,0:T(8,128)} %all-reduce.3.cloned.1.call-done) | copy-start | bytes 4718596
  158.4 41.6 %all-to-all-start.2 = ((f32[16,80,128]{2,1,0:T(8,128)}), f32[16,80,128]{2,1,0:T(8,128)S(1)}, u32[]{:S(2)}, u32[]{:S(2)}) async-start(f32[16,80,128]{2,1,0:T(8,128)} %select_divide_fusion), calls=%async_computation.2 | async-start | bytes 1310720 | tf_op jit(solution)/shard_map/all_to_all | solution.py:35
Sparse Core Ops, SparseCore 0:
  89.9 61.7 all-reduce.2
where the time goes:
time: 212 us; the launch traced here: 208 us
  waiting for transfers between devices  69.5 us (33%)
  local copies, waits for them, and re-layouts  58.1 us (27%)
  other arithmetic  26.6 us (13%)
  starting transfers between devices  21.8 us (10%)
  matrix products  16.5 us (8%)
  between operations  16.1 us (8%)
    psum x1, waiting for transfers between devices, regather(): region = lax.psum(empty.at[local].add(flat_vals, mode='drop'), 'group')  60.6 us
    reshape x1, local copies, waits for them, and re-layouts, body(): blocks = full.reshape(nblocks, 128)  18 us
    dot_general x1, matrix products, body(): jnp.einsum('td,te->de', acts, grad_out, preferred_element_type=jnp.float32)  16.5 us
    convert_element_type x1, local copies, waits for them, and re-layouts, body(): blocks.at[ids].set(0.0).reshape(width, width).astype(jnp.bfloat16)  13.3 us
    scatter x1, local copies, waits for them, and re-layouts, body(): blocks.at[ids].set(0.0).reshape(width, width).astype(jnp.bfloat16)  12.8 us
    scatter-add x1, other arithmetic, regather(): region = lax.psum(empty.at[local].add(flat_vals, mode='drop'), 'group')  10.1 us
    convert_element_type x1, other arithmetic, body(): blocks.at[ids].set(0.0).reshape(width, width).astype(jnp.bfloat16)  8.9 us
    all_to_all x1, waiting for transfers between devices, regather(): lax.all_to_all(send_vals, 'dp', split_axis=0, concat_axis=0, tiled=True)  8.88 us
  transfers between devices with their start and end apart: 4, of which 2 were waited for; matrix products, arithmetic and copies ran while one was open for 37% of the time, Pallas kernels for 0%

commit v1 on v0

v1 whole, which is shorter than its diff:
```python
import functools

import jax
import jax.numpy as jnp
from jax import lax
from jax.experimental import pallas as pl
from jax.experimental.pallas import tpu as pltpu
from jax.sharding import PartitionSpec as P

MESH = pl.DeviceIdType.MESH
CAP = 80
SUB = 8
ROWS = CAP // SUB
LANES = 128
WIDE = LANES // SUB
F32, BF16, I32 = jnp.float32, jnp.bfloat16, jnp.int32


def iota(shape, dim):
    return lax.broadcasted_iota(I32, shape, dim)


def onehot(mask):
    return jnp.where(mask, 1.0, 0.0).astype(BF16)


def dot(a, b, ca, cb):
    return lax.dot_general(a, b, (((ca,), (cb,)), ((), ())), preferred_element_type=F32)


def split(x):
    hi = x.astype(BF16)
    return hi, (x - hi.astype(F32)).astype(BF16)


def swap_blocks(x):
    n = x.shape[0]
    row = iota(x.shape, 0) & 7
    blk = iota(x.shape, 1) // WIDE
    for k in (1, 2, 4):
        low_row = (row & k) == 0
        low_blk = (blk & k) == 0
        up = pltpu.roll(pltpu.roll(x, n - k, 0), k * WIDE, 1)
        down = pltpu.roll(pltpu.roll(x, k, 0), LANES - k * WIDE, 1)
        x = jnp.where(low_row == low_blk, x, jnp.where(low_row, up, down))
    return x


def grads_kernel(
    keep, owners, acts, grad, err, kept_v, kept_s, bounds, out, send, pos_out, acc, ids_s, vals
):
    step = pl.program_id(0)
    steps = pl.num_programs(0)
    tile, width = err.shape
    pad = ids_s.shape[1]
    per_row = width // LANES

    @pl.when(step == 0)
    def _():
        ids_s[...] = jnp.full(ids_s.shape, -1, I32)
        ids_s[0:1, 0:keep] = kept_v[...]
        vals[...] = jnp.zeros(vals.shape, F32)

    ids = ids_s[0:1, :]
    live = ids >= 0
    full = dot(acts[...], grad[...], 0, 0) + err[...].astype(F32)
    hit_row = onehot((iota((tile, pad), 0) + step * tile == ids // per_row) & live)
    hit_col = onehot((iota((LANES, pad), 0) == ids % per_row) & live)
    cleared = dot(hit_row, hit_col, 1, 1)
    for c in range(per_row):
        block = full[:, c * LANES : (c + 1) * LANES]
        acc[c, pl.ds(step * tile, tile), :] = block
        out[:, c * LANES : (c + 1) * LANES] = jnp.where(
            cleared[:, c : c + 1] > 0.5, 0.0, block
        ).astype(BF16)

    @pl.when(step == steps - 1)
    def _():
        def take(k, carry):
            b = kept_s[0, k]
            vals[pl.ds(k, 1), :] = acc[b % per_row, pl.ds(b // per_row, 1), :]
            return carry

        lax.fori_loop(0, keep, take, 0, unroll=8)
        region = jnp.zeros(ids.shape, I32)
        for q in range(1, owners):
            region = region + (ids >= bounds[q]).astype(I32)
        of = (iota((owners, pad), 0) == region) & live
        earlier = onehot(iota((pad, pad), 0) < iota((pad, pad), 1))
        before = dot(onehot(of), earlier, 1, 0)
        slot = jnp.sum(jnp.where(of, before, 0.0), axis=0, keepdims=True).astype(I32)
        pos = jnp.where(live, region * CAP + slot, -1)
        pos_out[...] = jnp.broadcast_to(pos, pos_out.shape)
        at = onehot((iota((LANES, pad), 0) == slot) & live)
        high = jnp.where(of, (ids // 256).astype(F32), 0.0).astype(BF16)
        low = jnp.where(of, (ids % 256).astype(F32), 0.0).astype(BF16)
        number = dot(high, at, 1, 1) * 256.0 + dot(low, at, 1, 1)
        number = jnp.where(dot(onehot(of), at, 1, 1) > 0.5, number, -1048576.0)
        place = onehot((iota((owners * CAP, pad), 0) == pos) & live)
        hi, lo = split(vals[...])
        packed = swap_blocks(dot(place, hi, 1, 0) + dot(place, lo, 1, 0))
        for r in range(owners):
            for i in range(ROWS):
                tile_at = (r * ROWS + i) * SUB
                send[i, r * SUB : (r + 1) * SUB, :] = packed[tile_at : tile_at + SUB]
            send[ROWS, r * SUB : (r + 1) * SUB, :] = jnp.broadcast_to(
                number[r : r + 1, :], (SUB, LANES)
            )


def sums_kernel(groups, owners, bounds, send, back, got, oh, ans, ct, total, sems, bsem):
    g = lax.axis_index("group")
    d = lax.axis_index("dp")
    n = groups * owners
    me = g * owners + d
    home = d * groups + g
    heights = oh.shape[1]

    barrier = pltpu.get_barrier_semaphore()
    for i in range(1, groups):
        pl.semaphore_signal(
            barrier, inc=1, device_id=(lax.rem(g + i, groups), d), device_id_type=MESH
        )
    for i in range(1, owners):
        pl.semaphore_signal(
            barrier, inc=1, device_id=(g, lax.rem(d + i, owners)), device_id_type=MESH
        )
    pl.semaphore_wait(barrier, groups + owners - 2)
    for i in range(1, groups):
        pl.semaphore_signal(
            bsem, inc=1, device_id=(lax.rem(g + i, groups), d), device_id_type=MESH
        )
    pl.semaphore_wait(bsem, groups - 1)

    own = pltpu.make_async_copy(send.at[:, home, :], got.at[:, me, :], sems.at[4])
    own.start()

    def push(i, carry):
        tg = lax.rem(g + i // owners, groups)
        td = lax.rem(d + i % owners, owners)
        pltpu.make_async_remote_copy(
            src_ref=send.at[:, td * groups + tg, :],
            dst_ref=got.at[:, me, :],
            send_sem=sems.at[0],
            recv_sem=sems.at[1],
            device_id=(tg, td),
            device_id_type=MESH,
        ).start()
        return carry

    lax.fori_loop(1, n, push, 0)
    own.wait()
    most = got.at[:, pl.ds(0, n - 1), :]
    pltpu.make_async_copy(most, most, sems.at[1]).wait()
    pltpu.make_async_copy(most, most, sems.at[0]).wait()

    local = got[ROWS].T.astype(I32) - bounds[d]
    ct[0] = local >> 3
    ct[1] = local & 7
    total[...] = jnp.zeros(total.shape, F32)

    def add(i, carry):
        x = got[i].T
        hi = x.astype(BF16)
        hi, lo = hi.astype(F32), x - hi.astype(F32)
        high = ct[0, pl.ds(pl.multiple_of(i * SUB, SUB), SUB), :]
        low = ct[1, pl.ds(pl.multiple_of(i * SUB, SUB), SUB), :]
        parts = []
        for j in range(SUB):
            oh[i, :, j * n : (j + 1) * n] = onehot(iota((heights, n), 0) == high[j : j + 1, :])
            mine = [low[j : j + 1, :] == c for c in range(SUB)]
            rows = slice(j * WIDE, (j + 1) * WIDE)
            parts.append(
                jnp.concatenate(
                    [jnp.where(m, hi[rows], 0.0).astype(BF16) for m in mine]
                    + [jnp.where(m, lo[rows], 0.0).astype(BF16) for m in mine],
                    axis=0,
                )
            )
        total[...] += dot(oh[i], jnp.concatenate(parts, axis=1), 1, 1)
        return carry

    lax.fori_loop(0, ROWS, add, 0)
    whole = total[:, :LANES] + total[:, LANES:]
    ans[ROWS] = jnp.broadcast_to(jnp.sum(whole * whole, keepdims=True), (n, LANES))
    hi, lo = split(whole.T)
    table = jnp.concatenate([hi, lo], axis=0)

    def look(i, carry):
        both = dot(table, oh[i], 1, 0)
        both = both[:LANES] + both[LANES:]
        low = ct[1, pl.ds(pl.multiple_of(i * SUB, SUB), SUB), :]
        parts = []
        for j in range(SUB):
            picked = jnp.zeros((WIDE, n), F32)
            for c in range(SUB):
                picked = jnp.where(
                    low[j : j + 1, :] == c,
                    both[c * WIDE : (c + 1) * WIDE, j * n : (j + 1) * n],
                    picked,
                )
            parts.append(picked)
        ans[i] = jnp.concatenate(parts, axis=0).T
        return carry

    lax.fori_loop(0, ROWS, look, 0)

    own = pltpu.make_async_copy(ans.at[:, me, :], back.at[:, home, :], sems.at[4])
    own.start()

    def answer(i, carry):
        tg = lax.rem(g + i // owners, groups)
        td = lax.rem(d + i % owners, owners)
        pltpu.make_async_remote_copy(
            src_ref=ans.at[:, tg * owners + td, :],
            dst_ref=back.at[:, home, :],
            send_sem=sems.at[2],
            recv_sem=sems.at[3],
            device_id=(tg, td),
            device_id_type=MESH,
        ).start()
        return carry

    lax.fori_loop(1, n, answer, 0)
    own.wait()
    most = back.at[:, pl.ds(0, n - 1), :]
    pltpu.make_async_copy(most, most, sems.at[3]).wait()
    pltpu.make_async_copy(most, most, sems.at[2]).wait()


def finish_kernel(keep, owners, bounds, pos, back, out, slots):
    for r in range(owners):
        rows = slice(r * SUB, (r + 1) * SUB)
        square = jnp.sum(back[ROWS, rows, :], axis=0, keepdims=True)
        extent = jnp.full((1, LANES), bounds[r + 1] - bounds[r], I32).astype(F32)
        rms = jnp.sqrt(square / (extent * 128.0) + 1e-06)
        for i in range(ROWS):
            at = (r * ROWS + i) * SUB
            slots[at : at + SUB, :] = back[i, rows, :] / rms
    slots[...] = swap_blocks(slots[...])

    def take(k, carry):
        out[pl.ds(k, 1), :] = slots[pl.ds(pos[0, k], 1), :]
        return carry

    lax.fori_loop(0, keep, take, 0, unroll=8)


def body(groups, owners, acts, grad_out, error_in, kept, bounds):
    tokens, width = acts.shape
    keep = kept.shape[1]
    pad = -(-keep // LANES) * LANES
    n = groups * owners
    nblocks = width * width // LANES
    base = nblocks // owners
    heights = (base + 2 * (base // 4)) // SUB
    tile = 256
    smem = pl.BlockSpec(memory_space=pltpu.SMEM)
    vmem = pl.BlockSpec(memory_space=pltpu.VMEM)
    new_error, send, pos = pl.pallas_call(
        functools.partial(grads_kernel, keep, owners),
        grid=(width // tile,),
        in_specs=[
            pl.BlockSpec((tokens, tile), lambda i: (0, i)),
            pl.BlockSpec((tokens, width), lambda i: (0, 0)),
            pl.BlockSpec((tile, width), lambda i: (i, 0)),
            pl.BlockSpec((1, keep), lambda i: (0, 0)),
            smem,
            smem,
        ],
        out_specs=[
            pl.BlockSpec((tile, width), lambda i: (i, 0)),
            pl.BlockSpec((ROWS + 1, n, LANES), lambda i: (0, 0, 0)),
            pl.BlockSpec((8, pad), lambda i: (0, 0)),
        ],
        out_shape=[
            jax.ShapeDtypeStruct((width, width), BF16),
            jax.ShapeDtypeStruct((ROWS + 1, n, LANES), F32),
            jax.ShapeDtypeStruct((8, pad), I32),
        ],
        scratch_shapes=[
            pltpu.VMEM((width // LANES, width, LANES), F32),
            pltpu.VMEM((8, pad), I32),
            pltpu.VMEM((pad, LANES), F32),
        ],
        compiler_params=pltpu.CompilerParams(vmem_limit_bytes=56 << 20),
    )(acts, grad_out, error_in, kept, kept, bounds)
    back = pl.pallas_call(
        functools.partial(sums_kernel, groups, owners),
        in_specs=[smem, vmem],
        out_specs=vmem,
        out_shape=jax.ShapeDtypeStruct((ROWS + 1, n, LANES), F32),
        scratch_shapes=[
            pltpu.VMEM((ROWS + 1, n, LANES), F32),
            pltpu.VMEM((ROWS, heights, SUB * n), BF16),
            pltpu.VMEM((ROWS + 1, n, LANES), F32),
            pltpu.VMEM((2, LANES, n), I32),
            pltpu.VMEM((heights, 2 * LANES), F32),
            pltpu.SemaphoreType.DMA((5,)),
            pltpu.SemaphoreType.REGULAR,
        ],
        compiler_params=pltpu.CompilerParams(
            collective_id=0, has_side_effects=True, vmem_limit_bytes=40 << 20
        ),
    )(bounds, send)
    result = pl.pallas_call(
        functools.partial(finish_kernel, keep, owners),
        in_specs=[smem, smem, vmem],
        out_specs=vmem,
        out_shape=jax.ShapeDtypeStruct((keep, LANES), F32),
        scratch_shapes=[pltpu.VMEM((owners * CAP, LANES), F32)],
        compiler_params=pltpu.CompilerParams(vmem_limit_bytes=40 << 20),
    )(bounds, pos, back)
    return new_error, result[None]


def solution(mesh):
    spec = P(("group", "dp"), None)
    return jax.shard_map(
        functools.partial(body, mesh.shape["group"], mesh.shape["dp"]),
        mesh=mesh,
        in_specs=(spec, spec, spec, spec, P()),
        out_specs=(spec, P(("group", "dp"), None, None)),
        check_vma=False,
    )
```

time: 212 us -> 77.4 us (0.37); the launches traced: 208 us -> 77.2 us
  Pallas kernels: 0 us -> 74.7 us
  waiting for transfers between devices: 69.5 us -> 0 us
  local copies, waits for them, and re-layouts: 58.1 us -> 1.81 us
  other arithmetic: 26.6 us -> 0 us
  starting transfers between devices: 21.8 us -> 0 us
  matrix products: 16.5 us -> 0 us
  between operations: 16.1 us -> 0.67 us
    pallas_call x0 -> x3, Pallas kernels: none -> 74.7 us  [the longest x1 46.6 us: body(): pl.pallas_call(functools.partial(sums_kernel, groups, owners), in_specs=[...]
    psum x1 -> x0, waiting for transfers between devices: 60.6 us -> none  [regather(): region = lax.psum(empty.at[local].add(flat_vals, mode='drop'), 'group')]
    all_to_all x3 -> x0, starting transfers between devices: 21.7 us -> none  [the longest x1 8.43 us: regather(): lax.all_to_all(send_ids, 'dp', split_axis=0, concat_axis=0, tiled=True)]
    scatter x3 -> x0, local copies, waits for them, and re-layouts: 19.9 us -> none  [the longest x1 12.8 us: body(): blocks.at[ids].set(0.0).reshape(width, width).astype(jnp.bfloat16)]
    reshape x1 -> x0, local copies, waits for them, and re-layouts: 18 us -> none  [body(): blocks = full.reshape(nblocks, 128)]
    dot_general x1 -> x0, matrix products: 16.5 us -> none  [body(): jnp.einsum('td,te->de', acts, grad_out, preferred_element_type=jnp.float32)]
    convert_element_type x1 -> x0, local copies, waits for them, and re-layouts: 13.3 us -> none  [body(): blocks.at[ids].set(0.0).reshape(width, width).astype(jnp.bfloat16)]
    scatter-add x1 -> x0, other arithmetic: 10.1 us -> none  [regather(): region = lax.psum(empty.at[local].add(flat_vals, mode='drop'), 'group')]
  transfers between devices with their start and end apart: 4 -> 0, of which waited for: 2 -> 0; matrix products, arithmetic and copies ran while one was open for 37% -> 0% of each run, Pallas kernels for 0% -> 0%
where the time goes in v1:
time: 77.4 us; the launch traced here: 77.2 us
  Pallas kernels  74.7 us (97%)
  local copies, waits for them, and re-layouts  1.81 us (2%)
    pallas_call x1, Pallas kernels, body(): pl.pallas_call(functools.partial(sums_kernel, groups, owners), in_specs=[...  46.6 us
    pallas_call x1, Pallas kernels, body(): pl.pallas_call(functools.partial(grads_kernel, keep, owners), grid=(width...  24.8 us
    pallas_call x1, Pallas kernels, body(): pl.pallas_call(functools.partial(finish_kernel, keep, owners), in_specs=[...  3.33 us
    unnamed x6, local copies, waits for them, and re-layouts  1.81 us

profile of v1, /device:TPU:1, one launch (start us, length us, event | category | flops | bytes accessed | tf_op | source)
XLA Modules:
  0.0 77.2 jit_solution(11462343593533527780)
XLA Ops:
  0.6 0.0 copy-start.2
  0.6 24.8 %shard_map.68 = (bf16[2048,2048]{1,0:T(8,128)(2,1)}, f32[11,128,128]{2,1,0:T(8,128)}, s32[8,384]{1,0:T(8,128)}) custom-call(bf16[1024,2048]{1,0:T(8,128)(2,1)} %acts.1, bf16[1024,2048]{1,0:T(8,128)(2,1)} %grad.1, bf16[2048,2048]{1,0:T(8,128)(2,1)} %err.1, s32[1,328]{1,0:T(1,128)} %kept_s.1, s32[1,328]{1,0:T(1,128)} %kept_s.1, s32[17]{0:T(128)} %bounds.5), custom_call_target="tpu_custom_call" | custom-call | tf_op jit(solution)/shard_map/pallas_call | solution.py:260
  25.4 0.0 copy-done.2
  25.4 0.0 copy-start
  25.5 1.1 %copy-done = f32[11,128,128]{2,1,0:T(8,128)S(1)} copy-done((f32[11,128,128]{2,1,0:T(8,128)S(1)}, f32[11,128,128]{2,1,0:T(8,128)}, u32[]{:S(2)}) %copy-start) | copy-done | bytes 720920
  26.6 46.6 %shard_map.69.back = f32[11,128,128]{2,1,0:T(8,128)S(1)} custom-call(s32[17]{0:T(128)S(1)} %copy-done.2, f32[11,128,128]{2,1,0:T(8,128)S(1)} %copy-done), custom_call_target="tpu_custom_call" | custom-call | tf_op jit(solution)/shard_map/pallas_call | solution.py:288
  73.1 0.0 copy-start.1
  73.1 0.7 copy-done.1
  73.8 3.3 %shard_map.70 = f32[328,128]{1,0:T(8,128)} custom-call(s32[17]{0:T(128)S(1)} %copy-done.2, s32[8,384]{1,0:T(8,128)S(1)} %copy-done.1, f32[11,128,128]{2,1,0:T(8,128)S(1)} %shard_map.69.back), custom_call_target="tpu_custom_call" | custom-call | tf_op jit(solution)/shard_map/pallas_call | solution.py:306
Async XLA Ops:
  0.6 24.8 %copy-start.2 = (s32[17]{0:T(128)S(1)}, s32[17]{0:T(128)}, u32[]{:S(2)}) copy-start(s32[17]{0:T(128)} %bounds.5) | copy-start | bytes 208
  25.4 1.1 %copy-start = (f32[11,128,128]{2,1,0:T(8,128)S(1)}, f32[11,128,128]{2,1,0:T(8,128)}, u32[]{:S(2)}) copy-start(f32[11,128,128]{2,1,0:T(8,128)} %get-tuple-element.7.send) | copy-start | bytes 2162692
  73.1 0.7 copy-start.1

commit v2 on v0

v2 whole, which is shorter than its diff:
```python
import functools

import jax
import jax.numpy as jnp
from jax import lax
from jax.experimental import pallas as pl
from jax.experimental.pallas import tpu as pltpu
from jax.sharding import PartitionSpec as P

MESH = pl.DeviceIdType.MESH
CAP = 80
SUB = 8
ROWS = CAP // SUB
LANES = 128
WIDE = LANES // SUB
F32, BF16, I32 = jnp.float32, jnp.bfloat16, jnp.int32


def iota(shape, dim):
    return lax.broadcasted_iota(I32, shape, dim)


def onehot(mask):
    return jnp.where(mask, 1.0, 0.0).astype(BF16)


def dot(a, b, ca, cb):
    return lax.dot_general(a, b, (((ca,), (cb,)), ((), ())), preferred_element_type=F32)


def split(x):
    hi = x.astype(BF16)
    return hi, (x - hi.astype(F32)).astype(BF16)


def swap_blocks(x):
    n = x.shape[0]
    row = iota(x.shape, 0) & 7
    blk = iota(x.shape, 1) // WIDE
    for k in (1, 2, 4):
        low_row = (row & k) == 0
        low_blk = (blk & k) == 0
        up = pltpu.roll(pltpu.roll(x, n - k, 0), k * WIDE, 1)
        down = pltpu.roll(pltpu.roll(x, k, 0), LANES - k * WIDE, 1)
        x = jnp.where(low_row == low_blk, x, jnp.where(low_row, up, down))
    return x


def sums_kernel(
    keep, groups, owners, kept, bounds, acts_in, grad_in, err_in,
    err_out, back, pos_out,
    acts, grad, err, ids_s, rows_of, sel, packed, send, got, oh, ans, ct, total, sems, bsem,
):
    g = lax.axis_index("group")
    d = lax.axis_index("dp")
    n = groups * owners
    home = d * groups + g
    heights = oh.shape[1]
    width = err.shape[1]
    pad = ids_s.shape[1]
    half = n // 2
    tile = 256
    shift = (width // LANES).bit_length() - 1
    per_row = width // LANES

    loads = [
        pltpu.make_async_copy(a, b, sems.at[8 + i])
        for i, (a, b) in enumerate(((acts_in, acts), (grad_in, grad), (err_in, err)))
    ]
    for load in loads:
        load.start()
    barrier = pltpu.get_barrier_semaphore()
    for i in range(1, groups):
        pl.semaphore_signal(
            barrier, inc=1, device_id=(lax.rem(g + i, groups), d), device_id_type=MESH
        )
    for i in range(1, owners):
        pl.semaphore_signal(
            barrier, inc=1, device_id=(g, lax.rem(d + i, owners)), device_id_type=MESH
        )

    ids_s[...] = jnp.full(ids_s.shape, -1, I32)
    ids_s[0:1, 0:keep] = kept[...]
    ids = ids_s[0:1, :]
    live = ids >= 0
    idf = ids.astype(F32)
    column = jnp.concatenate(
        [
            jnp.broadcast_to(idf[:, b : b + LANES], (LANES, LANES)).T
            for b in range(0, pad, LANES)
        ],
        axis=0,
    ).astype(I32)
    rho = column >> shift
    kappa = column & (per_row - 1)
    for c in range(per_row):
        rows_of[:, c * LANES : (c + 1) * LANES] = onehot(
            iota((pad, LANES), 1) + c * LANES == rho
        )
    region = jnp.zeros(ids.shape, I32)
    for q in range(1, owners):
        region = region + (ids >= bounds[q]).astype(I32)
    of = (iota((owners, pad), 0) == region) & live
    earlier = onehot(iota((pad, pad), 0) < iota((pad, pad), 1))
    before = dot(onehot(of), earlier, 1, 0)
    slot = jnp.sum(jnp.where(of, before, 0.0), axis=0, keepdims=True).astype(I32)
    pos = jnp.where(live, region * CAP + slot, -1)
    pos_out[...] = jnp.broadcast_to(pos, pos_out.shape)
    at = onehot((iota((LANES, pad), 0) == slot) & live)
    high = jnp.where(of, (ids >> 8).astype(F32), 0.0).astype(BF16)
    low = jnp.where(of, (ids & 255).astype(F32), 0.0).astype(BF16)
    number = dot(high, at, 1, 1) * 256.0 + dot(low, at, 1, 1)
    number = jnp.where(dot(onehot(of), at, 1, 1) > 0.5, number, -1048576.0)

    loads[0].wait()
    sel[...] = dot(rows_of[...], acts[...], 1, 1).astype(BF16)
    pl.semaphore_wait(barrier, groups + owners - 2)
    for i in range(1, groups):
        pl.semaphore_signal(
            bsem, inc=1, device_id=(lax.rem(g + i, groups), d), device_id_type=MESH
        )
    loads[1].wait()
    loads[2].wait()
    vals = jnp.zeros((pad, LANES), F32)
    for c in range(0, width, 4 * LANES):
        cols = slice(c, c + 4 * LANES)
        part = dot(sel[...], grad[:, cols], 1, 0) + dot(rows_of[...], err[:, cols], 1, 0)
        for b in range(4):
            vals = jnp.where(
                kappa == c // LANES + b, part[:, b * LANES : (b + 1) * LANES], vals
            )
    place = onehot((iota((owners * CAP, pad), 0) == pos) & live)
    hi, lo = split(vals)
    packed[...] = swap_blocks(dot(place, hi, 1, 0) + dot(place, lo, 1, 0))
    for r in range(owners):
        for i in range(ROWS):
            tile_at = (r * ROWS + i) * SUB
            send[i, r * SUB : (r + 1) * SUB, :] = packed[tile_at : tile_at + SUB]
        send[ROWS, r * SUB : (r + 1) * SUB, :] = jnp.broadcast_to(
            number[r : r + 1, :], (SUB, LANES)
        )
    pl.semaphore_wait(bsem, groups - 1)

    own = pltpu.make_async_copy(send.at[:, home, :], got.at[:, 0, :], sems.at[6])
    own.start()

    def push(part):
        def one(o, carry):
            tg = lax.rem(g + o // owners, groups)
            td = lax.rem(d + o % owners, owners)
            pltpu.make_async_remote_copy(
                src_ref=send.at[:, td * groups + tg, :],
                dst_ref=got.at[:, o, :],
                send_sem=sems.at[0],
                recv_sem=sems.at[1 + part],
                device_id=(tg, td),
                device_id_type=MESH,
            ).start()
            return carry

        return one

    lax.fori_loop(1, half, push(0), 0)
    lax.fori_loop(half, n, push(1), 0)

    def product(t, carry):
        rows = pl.ds(pl.multiple_of(t * tile, tile), tile)
        hit_row = onehot(iota((tile, pad), 0) + t * tile == ids_s[0:1, :] >> shift)
        hit_col = onehot(iota((LANES, pad), 0) == ids_s[0:1, :] & (per_row - 1))
        cleared = dot(hit_row, hit_col, 1, 1)
        for c in range(0, width, 2 * LANES):
            cols = slice(c, c + 2 * LANES)
            full = dot(acts[:, rows], grad[:, cols], 0, 0) + err[rows, cols].astype(F32)
            for b in range(2):
                at_c = c // LANES + b
                err[rows, at_c * LANES : (at_c + 1) * LANES] = jnp.where(
                    cleared[:, at_c : at_c + 1] > 0.5, 0.0, full[:, b * LANES : (b + 1) * LANES]
                ).astype(BF16)
        return carry

    first = width // tile // 2
    lax.fori_loop(0, first, product, 0)
    upper = pl.ds(0, first * tile)
    stores = [pltpu.make_async_copy(err.at[upper], err_out.at[upper], sems.at[7])]
    stores[0].start()

    total[...] = jnp.zeros(total.shape, F32)
    left = iota((SUB, LANES), 1) < half

    def index_rows(h, p, which):
        at_p = pl.multiple_of(p * 2 * SUB, 2 * SUB)
        return jnp.where(
            left, ct[h, which, pl.ds(at_p, SUB), :], ct[h, which, pl.ds(at_p + SUB, SUB), :]
        )

    def add(h):
        def one(p, carry):
            x = jnp.concatenate(
                [
                    got[2 * p, h * half : (h + 1) * half, :],
                    got[2 * p + 1, h * half : (h + 1) * half, :],
                ],
                axis=0,
            ).T
            hi = x.astype(BF16).astype(F32)
            lo = x - hi
            high = index_rows(h, p, 0)
            low = index_rows(h, p, 1)
            step = h * (ROWS // 2) + p
            parts = []
            for j in range(SUB):
                oh[step, :, j * n : (j + 1) * n] = onehot(
                    iota((heights, n), 0) == high[j : j + 1, :]
                )
                mine = [low[j : j + 1, :] == c for c in range(SUB)]
                rows = slice(j * WIDE, (j + 1) * WIDE)
                parts.append(
                    jnp.concatenate(
                        [jnp.where(m, hi[rows], 0.0).astype(BF16) for m in mine]
                        + [jnp.where(m, lo[rows], 0.0).astype(BF16) for m in mine],
                        axis=0,
                    )
                )
            total[...] += dot(oh[step], jnp.concatenate(parts, axis=1), 1, 1)
            return carry

        return one

    own.wait()
    for h in range(2):
        arrived = got.at[:, pl.ds(0, half - 1 + h), :]
        pltpu.make_async_copy(arrived, arrived, sems.at[1 + h]).wait()
        numbers = got[ROWS, h * half : (h + 1) * half, :]
        local = jnp.concatenate([numbers, numbers], axis=0).T.astype(I32) - bounds[d]
        ct[h, 0] = local >> 3
        ct[h, 1] = local & 7
        lax.fori_loop(0, ROWS // 2, add(h), 0)

    whole = total[:, :LANES] + total[:, LANES:]
    ans[ROWS] = jnp.broadcast_to(jnp.sum(whole * whole, keepdims=True), (n, LANES))
    hi, lo = split(whole.T)
    table = jnp.concatenate([hi, lo], axis=0)

    def look(h):
        def one(p, carry):
            both = dot(table, oh[h * (ROWS // 2) + p], 1, 0)
            both = both[:LANES] + both[LANES:]
            low = index_rows(h, p, 1)
            parts = []
            for j in range(SUB):
                picked = jnp.zeros((WIDE, n), F32)
                for c in range(SUB):
                    picked = jnp.where(
                        low[j : j + 1, :] == c,
                        both[c * WIDE : (c + 1) * WIDE, j * n : (j + 1) * n],
                        picked,
                    )
                parts.append(picked)
            rows = jnp.concatenate(parts, axis=0).T
            ans[2 * p, h * half : (h + 1) * half, :] = rows[:half]
            ans[2 * p + 1, h * half : (h + 1) * half, :] = rows[half:]
            return carry

        return one

    def answer(o, carry):
        tg = lax.rem(g + groups - o // owners, groups)
        td = lax.rem(d + owners - o % owners, owners)
        pltpu.make_async_remote_copy(
            src_ref=ans.at[:, o, :],
            dst_ref=back.at[:, home, :],
            send_sem=sems.at[4],
            recv_sem=sems.at[5],
            device_id=(tg, td),
            device_id_type=MESH,
        ).start()
        return carry

    lax.fori_loop(0, ROWS // 2, look(0), 0)
    own = pltpu.make_async_copy(ans.at[:, 0, :], back.at[:, home, :], sems.at[6])
    own.start()
    lax.fori_loop(1, half, answer, 0)
    lax.fori_loop(0, ROWS // 2, look(1), 0)
    lax.fori_loop(half, n, answer, 0)

    lax.fori_loop(first, width // tile, product, 0)
    stores[0].wait()
    lower = pl.ds(first * tile, width - first * tile)
    stores.append(pltpu.make_async_copy(err.at[lower], err_out.at[lower], sems.at[7]))
    stores[1].start()
    own.wait()
    sent = got.at[:, pl.ds(0, n - 1), :]
    pltpu.make_async_copy(sent, sent, sems.at[0]).wait()
    pltpu.make_async_copy(sent, sent, sems.at[4]).wait()
    came = back.at[:, pl.ds(0, n - 1), :]
    pltpu.make_async_copy(came, came, sems.at[5]).wait()
    stores[1].wait()


def finish_kernel(keep, owners, bounds, pos, back, err_in, out, err_out, slots, held, sems):
    parts = sems.shape[1]
    rows = err_in.shape[0] // parts
    cuts = [pl.ds(i * rows, rows) for i in range(parts)]
    loads = [
        pltpu.make_async_copy(err_in.at[cut], held.at[cut], sems.at[0, i])
        for i, cut in enumerate(cuts)
    ]
    stores = [
        pltpu.make_async_copy(held.at[cut], err_out.at[cut], sems.at[1, i])
        for i, cut in enumerate(cuts)
    ]
    for load in loads:
        load.start()
    for r in range(owners):
        if r % 2 == 0:
            loads[r // 2].wait()
            stores[r // 2].start()
        rows = slice(r * SUB, (r + 1) * SUB)
        square = jnp.sum(back[ROWS, rows, :], axis=0, keepdims=True)
        extent = jnp.full((1, LANES), bounds[r + 1] - bounds[r], I32).astype(F32)
        rms = jnp.sqrt(square / (extent * 128.0) + 1e-06)
        for i in range(ROWS):
            at = (r * ROWS + i) * SUB
            slots[at : at + SUB, :] = back[i, rows, :] / rms
    slots[...] = swap_blocks(slots[...])

    def take(k, carry):
        out[pl.ds(k, 1), :] = slots[pl.ds(pos[0, k], 1), :]
        return carry

    lax.fori_loop(0, keep, take, 0, unroll=8)
    for store in stores:
        store.wait()


def body(groups, owners, acts, grad_out, error_in, kept, bounds):
    tokens, width = acts.shape
    keep = kept.shape[1]
    pad = -(-keep // LANES) * LANES
    n = groups * owners
    nblocks = width * width // LANES
    base = nblocks // owners
    heights = (base + 2 * (base // 4)) // SUB
    smem = pl.BlockSpec(memory_space=pltpu.SMEM)
    vmem = pl.BlockSpec(memory_space=pltpu.VMEM)
    hbm = pl.BlockSpec(memory_space=pl.ANY)
    new_error, back, pos = pl.pallas_call(
        functools.partial(sums_kernel, keep, groups, owners),
        in_specs=[vmem, smem, hbm, hbm, hbm],
        out_specs=[hbm, vmem, vmem],
        out_shape=[
            jax.ShapeDtypeStruct((width, width), BF16),
            jax.ShapeDtypeStruct((ROWS + 1, n, LANES), F32),
            jax.ShapeDtypeStruct((8, pad), I32),
        ],
        scratch_shapes=[
            pltpu.VMEM((tokens, width), BF16),
            pltpu.VMEM((tokens, width), BF16),
            pltpu.VMEM((width, width), BF16),
            pltpu.VMEM((8, pad), I32),
            pltpu.VMEM((pad, width), BF16),
            pltpu.VMEM((pad, tokens), BF16),
            pltpu.VMEM((owners * CAP, LANES), F32),
            pltpu.VMEM((ROWS + 1, n, LANES), F32),
            pltpu.VMEM((ROWS + 1, n, LANES), F32),
            pltpu.VMEM((ROWS, heights, SUB * n), BF16),
            pltpu.VMEM((ROWS + 1, n, LANES), F32),
            pltpu.VMEM((2, 2, LANES, n), I32),
            pltpu.VMEM((heights, 2 * LANES), F32),
            pltpu.SemaphoreType.DMA((11,)),
            pltpu.SemaphoreType.REGULAR,
        ],
        compiler_params=pltpu.CompilerParams(
            collective_id=0, has_side_effects=True, vmem_limit_bytes=60 << 20
        ),
    )(kept, bounds, acts, grad_out, error_in)
    result, new_error = pl.pallas_call(
        functools.partial(finish_kernel, keep, owners),
        in_specs=[smem, smem, vmem, hbm],
        out_specs=[vmem, hbm],
        out_shape=[
            jax.ShapeDtypeStruct((keep, LANES), F32),
            jax.ShapeDtypeStruct((width, width), BF16),
        ],
        scratch_shapes=[
            pltpu.VMEM((owners * CAP, LANES), F32),
            pltpu.VMEM((width, width), BF16),
            pltpu.SemaphoreType.DMA((2, owners // 2)),
        ],
        compiler_params=pltpu.CompilerParams(vmem_limit_bytes=60 << 20),
    )(bounds, pos, back, new_error)
    return new_error, result[None]


def solution(mesh):
    spec = P(("group", "dp"), None)
    return jax.shard_map(
        functools.partial(body, mesh.shape["group"], mesh.shape["dp"]),
        mesh=mesh,
        in_specs=(spec, spec, spec, spec, P()),
        out_specs=(spec, P(("group", "dp"), None, None)),
        check_vma=False,
    )
```

time: 212 us -> 62.2 us (0.29); the launches traced: 208 us -> 62 us
  waiting for transfers between devices: 69.5 us -> 0 us
  Pallas kernels: 0 us -> 61.2 us
  local copies, waits for them, and re-layouts: 58.1 us -> 0 us
  other arithmetic: 26.6 us -> 0 us
  starting transfers between devices: 21.8 us -> 0 us
  matrix products: 16.5 us -> 0 us
  between operations: 16.1 us -> 0.8 us
    pallas_call x0 -> x2, Pallas kernels: none -> 61.2 us  [the longest x1 52.2 us: body(): pl.pallas_call(functools.partial(sums_kernel, keep, groups, owners), in_s...]
    psum x1 -> x0, waiting for transfers between devices: 60.6 us -> none  [regather(): region = lax.psum(empty.at[local].add(flat_vals, mode='drop'), 'group')]
    all_to_all x3 -> x0, starting transfers between devices: 21.7 us -> none  [the longest x1 8.43 us: regather(): lax.all_to_all(send_ids, 'dp', split_axis=0, concat_axis=0, tiled=True)]
    scatter x3 -> x0, local copies, waits for them, and re-layouts: 19.9 us -> none  [the longest x1 12.8 us: body(): blocks.at[ids].set(0.0).reshape(width, width).astype(jnp.bfloat16)]
    reshape x1 -> x0, local copies, waits for them, and re-layouts: 18 us -> none  [body(): blocks = full.reshape(nblocks, 128)]
    dot_general x1 -> x0, matrix products: 16.5 us -> none  [body(): jnp.einsum('td,te->de', acts, grad_out, preferred_element_type=jnp.float32)]
    convert_element_type x1 -> x0, local copies, waits for them, and re-layouts: 13.3 us -> none  [body(): blocks.at[ids].set(0.0).reshape(width, width).astype(jnp.bfloat16)]
    scatter-add x1 -> x0, other arithmetic: 10.1 us -> none  [regather(): region = lax.psum(empty.at[local].add(flat_vals, mode='drop'), 'group')]
  transfers between devices with their start and end apart: 4 -> 0, of which waited for: 2 -> 0; matrix products, arithmetic and copies ran while one was open for 37% -> 0% of each run, Pallas kernels for 0% -> 0%
where the time goes in v2:
time: 62.2 us; the launch traced here: 62 us
  Pallas kernels  61.2 us (98%)
  between operations  0.8 us (1%)
    pallas_call x1, Pallas kernels, body(): pl.pallas_call(functools.partial(sums_kernel, keep, groups, owners), in_s...  52.2 us
    pallas_call x1, Pallas kernels, body(): pl.pallas_call(functools.partial(finish_kernel, keep, owners), in_specs=[...  9.08 us

profile of v2, /device:TPU:1, one launch (start us, length us, event | category | flops | bytes accessed | tf_op | source)
XLA Modules:
  0.0 62.0 jit_solution(7428995370954492013)
XLA Ops:
  0.6 52.2 %shard_map.68 = (bf16[2048,2048]{1,0:T(8,128)(2,1)}, f32[11,128,128]{2,1,0:T(8,128)}, s32[8,384]{1,0:T(8,128)}) custom-call(s32[1,328]{1,0:T(1,128)} %kept.1, s32[17]{0:T(128)} %bounds.3, bf16[1024,2048]{1,0:T(8,128)(2,1)} %acts_in.1, bf16[1024,2048]{1,0:T(8,128)(2,1)} %grad_in.1, bf16[2048,2048]{1,0:T(8,128)(2,1)} %err_in.1), custom_call_target="tpu_custom_call" | custom-call | tf_op jit(solution)/shard_map/pallas_call | solution.py:347
  52.8 9.1 %shard_map.69 = (f32[328,128]{1,0:T(8,128)}, bf16[2048,2048]{1,0:T(8,128)(2,1)}) custom-call(s32[17]{0:T(128)} %bounds.3, s32[8,384]{1,0:T(8,128)} %get-tuple-element.7.pos, f32[11,128,128]{2,1,0:T(8,128)} %get-tuple-element.8.back, bf16[2048,2048]{1,0:T(8,128)(2,1)} %get-tuple-element.9.err_in), custom_call_target="tpu_custom_call" | custom-call | tf_op jit(solution)/shard_map/pallas_call | solution.py:377

commit v3 on v2

v3 whole, which is shorter than its diff:
```python
import functools

import jax
import jax.numpy as jnp
from jax import lax
from jax.experimental import pallas as pl
from jax.experimental.pallas import tpu as pltpu
from jax.sharding import PartitionSpec as P

MESH = pl.DeviceIdType.MESH
CAP = 97
SUB = 16
ROWS = 6
LANES = 128
WIDE = LANES // SUB
LAST = (ROWS + 1) * SUB
F32, BF16, I32 = jnp.float32, jnp.bfloat16, jnp.int32


def iota(shape, dim):
    return lax.broadcasted_iota(I32, shape, dim)


def onehot(mask):
    return jnp.where(mask, 1.0, 0.0).astype(BF16)


def dot(a, b, ca, cb):
    return lax.dot_general(a, b, (((ca,), (cb,)), ((), ())), preferred_element_type=F32)


def split(x):
    hi = x.astype(BF16)
    return hi, (x - hi.astype(F32)).astype(BF16)


def swap_blocks(x):
    n = x.shape[0]
    row = iota(x.shape, 0) & (SUB - 1)
    blk = iota(x.shape, 1) // WIDE
    for k in (1, 2, 4, 8):
        low_row = (row & k) == 0
        low_blk = (blk & k) == 0
        up = pltpu.roll(pltpu.roll(x, n - k, 0), k * WIDE, 1)
        down = pltpu.roll(pltpu.roll(x, k, 0), LANES - k * WIDE, 1)
        x = jnp.where(low_row == low_blk, x, jnp.where(low_row, up, down))
    return x


def sums_kernel(
    keep, groups, owners, kept, bounds, acts_in, grad_in, err_in,
    err_out, back, pos_out,
    acts, grad, err, ids_s, rows_of, sel, kept_rows, packed, send, got, oh, oh_last, put, ans, ct,
    total, sems, bsem,
):
    g = lax.axis_index("group")
    d = lax.axis_index("dp")
    n = groups * owners
    me = g * owners + d
    heights = oh.shape[1]
    width = err.shape[1]
    pad = ids_s.shape[1]
    half = n // 2
    tile = 256
    shift = (width // LANES).bit_length() - 1
    per_row = width // LANES

    load_acts = pltpu.make_async_copy(acts_in, acts, sems.at[8])
    load_grad = pltpu.make_async_copy(grad_in, grad, sems.at[9])
    quarter = width // 4
    cuts = [pl.ds(i * quarter, quarter) for i in range(4)]
    load_err = [
        pltpu.make_async_copy(err_in.at[cut], err.at[cut], sems.at[10 + i])
        for i, cut in enumerate(cuts)
    ]
    load_acts.start()
    barrier = pltpu.get_barrier_semaphore()
    for i in range(1, groups):
        pl.semaphore_signal(
            barrier, inc=1, device_id=(lax.rem(g + i, groups), d), device_id_type=MESH
        )
    for i in range(1, owners):
        pl.semaphore_signal(
            barrier, inc=1, device_id=(g, lax.rem(d + i, owners)), device_id_type=MESH
        )

    ids_s[...] = jnp.full(ids_s.shape, -1, I32)
    ids_s[0:1, 0:keep] = kept[...]
    ids = ids_s[0:1, :]
    live = ids >= 0
    idf = ids.astype(F32)
    column = jnp.concatenate(
        [
            jnp.broadcast_to(idf[:, b : b + LANES], (LANES, LANES)).T
            for b in range(0, pad, LANES)
        ],
        axis=0,
    ).astype(I32)
    rho = column >> shift
    kappa = column & (per_row - 1)
    for c in range(per_row):
        rows_of[:, c * LANES : (c + 1) * LANES] = onehot(
            iota((pad, LANES), 1) + c * LANES == rho
        )
    load_grad.start()
    region = jnp.zeros(ids.shape, I32)
    for q in range(1, owners):
        region = region + (ids >= bounds[q]).astype(I32)
    of = (iota((groups, pad), 0) == region >> 1) & live
    earlier = onehot(iota((pad, pad), 0) < iota((pad, pad), 1))
    before = dot(onehot(of), earlier, 1, 0)
    slot = jnp.sum(jnp.where(of, before, 0.0), axis=0, keepdims=True).astype(I32)
    pos = (region >> 1) * LAST + slot + jnp.where(slot == CAP - 1, SUB - 1, 0)
    pos = jnp.where(live, pos, -1)
    pos_out[...] = jnp.broadcast_to(pos * owners + region, pos_out.shape)
    at = onehot((iota((LANES, pad), 0) == slot) & live)
    high = jnp.where(of, (ids >> 8).astype(F32), 0.0).astype(BF16)
    low = jnp.where(of, (ids & 255).astype(F32), 0.0).astype(BF16)
    number = dot(high, at, 1, 1) * 256.0 + dot(low, at, 1, 1)
    number = jnp.where(dot(onehot(of), at, 1, 1) > 0.5, number, -1048576.0)

    load_acts.wait()
    for load in load_err:
        load.start()
    sel[...] = dot(rows_of[...], acts[...], 1, 1).astype(BF16)
    pl.semaphore_wait(barrier, groups + owners - 2)
    for i in range(1, groups):
        pl.semaphore_signal(
            bsem, inc=1, device_id=(lax.rem(g + i, groups), d), device_id_type=MESH
        )
    load_grad.wait()
    kept_rows[...] = dot(sel[...], grad[...], 1, 0)
    for load, cut in zip(load_err[:-1], cuts):
        load.wait()
        kept_rows[...] += dot(rows_of[:, cut], err[cut, :], 1, 0)
    load_err[-1].wait()
    vals = jnp.zeros((pad, LANES), F32)
    for c in range(0, width, 4 * LANES):
        cols = slice(c, c + 4 * LANES)
        part = kept_rows[:, cols] + dot(rows_of[:, cuts[-1]], err[cuts[-1], cols], 1, 0)
        for b in range(4):
            vals = jnp.where(
                kappa == c // LANES + b, part[:, b * LANES : (b + 1) * LANES], vals
            )
    place = onehot((iota((groups * LAST, pad), 0) == pos) & live)
    hi, lo = split(vals)
    packed[...] = swap_blocks(dot(place, hi, 1, 0) + dot(place, lo, 1, 0))
    for q in range(groups):
        rows = slice(q * SUB, (q + 1) * SUB)
        for i in range(ROWS + 1):
            at_q = (q * (ROWS + 1) + i) * SUB
            block = packed[at_q : at_q + SUB]
            if i == ROWS:
                block = jnp.where(
                    iota((SUB, LANES), 1) < LANES - SUB,
                    jnp.broadcast_to(number[q : q + 1, :], (SUB, LANES)),
                    block,
                )
            send[i, rows, :] = block
    pl.semaphore_wait(bsem, groups - 1)

    own = pltpu.make_async_copy(send.at[:, me, :], got.at[:, 0, :], sems.at[6])
    own.start()

    def push(part):
        def one(o, carry):
            tg = lax.rem(g + o // owners, groups)
            td = lax.rem(d + o % owners, owners)
            pltpu.make_async_remote_copy(
                src_ref=send.at[:, tg * owners + td, :],
                dst_ref=got.at[:, o, :],
                send_sem=sems.at[0],
                recv_sem=sems.at[1 + part],
                device_id=(tg, td),
                device_id_type=MESH,
            ).start()
            return carry

        return one

    lax.fori_loop(1, half, push(0), 0)
    lax.fori_loop(half, n, push(1), 0)

    def product(t, carry):
        rows = pl.ds(pl.multiple_of(t * tile, tile), tile)
        hit_row = onehot(iota((tile, pad), 0) + t * tile == ids_s[0:1, :] >> shift)
        hit_col = onehot(iota((LANES, pad), 0) == ids_s[0:1, :] & (per_row - 1))
        cleared = dot(hit_row, hit_col, 1, 1)
        for c in range(0, width, 2 * LANES):
            cols = slice(c, c + 2 * LANES)
            full = dot(acts[:, rows], grad[:, cols], 0, 0) + err[rows, cols].astype(F32)
            for b in range(2):
                at_c = c // LANES + b
                err[rows, at_c * LANES : (at_c + 1) * LANES] = jnp.where(
                    cleared[:, at_c : at_c + 1] > 0.5, 0.0, full[:, b * LANES : (b + 1) * LANES]
                ).astype(BF16)
        return carry

    first = width // tile // 2
    lax.fori_loop(0, first, product, 0)
    upper = pl.ds(0, first * tile)
    stores = [pltpu.make_async_copy(err.at[upper], err_out.at[upper], sems.at[7])]
    stores[0].start()

    total[...] = jnp.zeros(total.shape, F32)
    left = iota((SUB, LANES), 1) < half
    def index_rows(h, p, which):
        at_p = pl.multiple_of(p * 2 * SUB, 2 * SUB)
        return jnp.where(
            left, ct[h, which, pl.ds(at_p, SUB), :], ct[h, which, pl.ds(at_p + SUB, SUB), :]
        )

    def height_of(row):
        return onehot(iota((heights, n), 0) == row)

    def put_of(row, x):
        hi = x.astype(BF16).astype(F32)
        mine = [row == c for c in range(SUB)]
        return [
            jnp.concatenate([jnp.where(m, part, 0.0) for m in mine], axis=0).astype(BF16)
            for part in (hi, x - hi)
        ]

    def add(h):
        def one(p, carry):
            x = jnp.concatenate(
                [
                    got[2 * p, h * half : (h + 1) * half, :],
                    got[2 * p + 1, h * half : (h + 1) * half, :],
                ],
                axis=0,
            ).T
            high = index_rows(h, p, 0)
            low = index_rows(h, p, 1)
            step = h * (ROWS // 2) + p
            for j in range(SUB):
                lanes = slice(j * n, (j + 1) * n)
                oh[step, :, lanes] = height_of(high[j : j + 1, :])
                hi, lo = put_of(low[j : j + 1, :], x[j * WIDE : (j + 1) * WIDE])
                put[:LANES, lanes] = hi
                put[LANES:, lanes] = lo
            total[...] += dot(oh[step], put[...], 1, 1)
            return carry

        return one

    own.wait()
    for h in range(2):
        arrived = got.at[:, pl.ds(0, half - 1 + h), :]
        pltpu.make_async_copy(arrived, arrived, sems.at[1 + h]).wait()
        numbers = got[ROWS, h * half : (h + 1) * half, :]
        local = jnp.concatenate([numbers, numbers], axis=0).T.astype(I32) - bounds[2 * g]
        ct[h, 0] = local >> 4
        ct[h, 1] = local & (SUB - 1)
        lax.fori_loop(0, ROWS // 2, add(h), 0)

    first_half = iota((1, n), 1) < half
    high, low = (
        jnp.where(first_half, ct[0, k, CAP - 1 : CAP, :], ct[1, k, CAP - 1 : CAP, :])
        for k in range(2)
    )
    oh_last[...] = height_of(high)
    parts = put_of(low, got[ROWS].T[LANES - WIDE :])
    total[...] += dot(oh_last[...], jnp.concatenate(parts, axis=0), 1, 1)

    whole = total[:, :LANES] + total[:, LANES:]
    square = whole * whole
    at_block = iota((heights, LANES), 0) * SUB + iota((heights, LANES), 1) // WIDE
    in_first = at_block < bounds[2 * g + 1] - bounds[2 * g]
    squares = [
        jnp.sum(jnp.where(in_first, square, 0.0), keepdims=True),
        jnp.sum(jnp.where(in_first, 0.0, square), keepdims=True),
    ]
    hi, lo = split(whole.T)
    table = jnp.concatenate([hi, lo], axis=0)

    def pick(both, row):
        picked = jnp.zeros((WIDE, n), F32)
        for c in range(SUB):
            picked = jnp.where(row == c, both[c * WIDE : (c + 1) * WIDE], picked)
        return picked

    both = dot(table, oh_last[...], 1, 0)
    last = pick(both[:LANES] + both[LANES:], low)
    last = jnp.concatenate([jnp.zeros((LANES - WIDE, n), F32), last], axis=0).T
    lane = iota((n, LANES), 1)
    ans[ROWS] = jnp.where(
        lane < LANES - SUB, jnp.where(lane < LANES // 2, squares[0], squares[1]), last
    )

    def look(h):
        def one(p, carry):
            both = dot(table, oh[h * (ROWS // 2) + p], 1, 0)
            both = both[:LANES] + both[LANES:]
            low = index_rows(h, p, 1)
            rows = jnp.concatenate(
                [pick(both[:, j * n : (j + 1) * n], low[j : j + 1, :]) for j in range(SUB)], axis=0
            ).T
            ans[2 * p, h * half : (h + 1) * half, :] = rows[:half]
            ans[2 * p + 1, h * half : (h + 1) * half, :] = rows[half:]
            return carry

        return one

    def answer(o, carry):
        tg = lax.rem(g + groups - o // owners, groups)
        td = lax.rem(d + owners - o % owners, owners)
        pltpu.make_async_remote_copy(
            src_ref=ans.at[:, o, :],
            dst_ref=back.at[:, me, :],
            send_sem=sems.at[4],
            recv_sem=sems.at[5],
            device_id=(tg, td),
            device_id_type=MESH,
        ).start()
        return carry

    lax.fori_loop(0, ROWS // 2, look(0), 0)
    own = pltpu.make_async_copy(ans.at[:, 0, :], back.at[:, me, :], sems.at[6])
    own.start()
    lax.fori_loop(1, half, answer, 0)
    lax.fori_loop(0, ROWS // 2, look(1), 0)
    lax.fori_loop(half, n, answer, 0)

    lax.fori_loop(first, width // tile, product, 0)
    stores[0].wait()
    lower = pl.ds(first * tile, width - first * tile)
    stores.append(pltpu.make_async_copy(err.at[lower], err_out.at[lower], sems.at[7]))
    stores[1].start()
    own.wait()
    sent = got.at[:, pl.ds(0, n - 1), :]
    pltpu.make_async_copy(sent, sent, sems.at[0]).wait()
    pltpu.make_async_copy(sent, sent, sems.at[4]).wait()
    came = back.at[:, pl.ds(0, n - 1), :]
    pltpu.make_async_copy(came, came, sems.at[5]).wait()
    stores[1].wait()


def finish_kernel(keep, groups, owners, bounds, pos, back, err_in, out, err_out, slots, scale, sem):
    store = pltpu.make_async_copy(err_in, err_out, sem)
    store.start()
    for q in range(groups):
        rows = slice(q * SUB, (q + 1) * SUB)
        square = jnp.sum(back[ROWS, rows, :], axis=0, keepdims=True)
        for k in range(2):
            r = 2 * q + k
            extent = jnp.full((1, LANES), bounds[r + 1] - bounds[r], I32).astype(F32)
            at = k * LANES // 2
            mean = jnp.broadcast_to(square[:, at : at + 1], (1, LANES)) / (extent * 128.0)
            scale[r : r + 1, :] = 1.0 / jnp.sqrt(mean + 1e-06)
        for i in range(ROWS + 1):
            at = (q * (ROWS + 1) + i) * SUB
            slots[at : at + SUB, :] = back[i, rows, :]
    slots[...] = swap_blocks(slots[...])

    def take(k, carry):
        at = pos[0, k]
        out[pl.ds(k, 1), :] = slots[pl.ds(at >> 4, 1), :] * scale[pl.ds(at & (owners - 1), 1), :]
        return carry

    lax.fori_loop(0, keep, take, 0, unroll=8)
    store.wait()


def body(groups, owners, acts, grad_out, error_in, kept, bounds):
    tokens, width = acts.shape
    keep = kept.shape[1]
    pad = -(-keep // LANES) * LANES
    n = groups * owners
    nblocks = width * width // LANES
    base = nblocks // owners
    heights = 2 * (base + 2 * (base // 4)) // SUB
    smem = pl.BlockSpec(memory_space=pltpu.SMEM)
    vmem = pl.BlockSpec(memory_space=pltpu.VMEM)
    hbm = pl.BlockSpec(memory_space=pl.ANY)
    new_error, back, pos = pl.pallas_call(
        functools.partial(sums_kernel, keep, groups, owners),
        in_specs=[vmem, smem, hbm, hbm, hbm],
        out_specs=[hbm, vmem, vmem],
        out_shape=[
            pltpu.VMEM((width, width), BF16),
            pltpu.VMEM((ROWS + 1, n, LANES), F32),
            pltpu.VMEM((8, pad), I32),
        ],
        scratch_shapes=[
            pltpu.VMEM((tokens, width), BF16),
            pltpu.VMEM((tokens, width), BF16),
            pltpu.VMEM((width, width), BF16),
            pltpu.VMEM((8, pad), I32),
            pltpu.VMEM((pad, width), BF16),
            pltpu.VMEM((pad, tokens), BF16),
            pltpu.VMEM((pad, width), F32),
            pltpu.VMEM((groups * LAST, LANES), F32),
            pltpu.VMEM((ROWS + 1, n, LANES), F32),
            pltpu.VMEM((ROWS + 1, n, LANES), F32),
            pltpu.VMEM((ROWS, heights, SUB * n), BF16),
            pltpu.VMEM((heights, n), BF16),
            pltpu.VMEM((2 * LANES, SUB * n), BF16),
            pltpu.VMEM((ROWS + 1, n, LANES), F32),
            pltpu.VMEM((2, 2, LANES, n), I32),
            pltpu.VMEM((heights, 2 * LANES), F32),
            pltpu.SemaphoreType.DMA((14,)),
            pltpu.SemaphoreType.REGULAR,
        ],
        compiler_params=pltpu.CompilerParams(
            collective_id=0, has_side_effects=True, vmem_limit_bytes=48 << 20
        ),
    )(*(pltpu.with_memory_space_constraint(x, pltpu.HBM) for x in (kept, bounds, acts, grad_out, error_in)))
    result, new_error = pl.pallas_call(
        functools.partial(finish_kernel, keep, groups, owners),
        in_specs=[smem, smem, vmem, hbm],
        out_specs=[vmem, hbm],
        out_shape=[
            jax.ShapeDtypeStruct((keep, LANES), F32),
            jax.ShapeDtypeStruct((width, width), BF16),
        ],
        scratch_shapes=[
            pltpu.VMEM((groups * LAST, LANES), F32),
            pltpu.VMEM((owners, LANES), F32),
            pltpu.SemaphoreType.DMA,
        ],
        compiler_params=pltpu.CompilerParams(vmem_limit_bytes=12 << 20),
    )(bounds, pos, back, new_error)
    return new_error, result[None]


def solution(mesh):
    spec = P(("group", "dp"), None)
    return jax.shard_map(
        functools.partial(body, mesh.shape["group"], mesh.shape["dp"]),
        mesh=mesh,
        in_specs=(spec, spec, spec, spec, P()),
        out_specs=(spec, P(("group", "dp"), None, None)),
        check_vma=False,
    )
```

time: 62.2 us -> 55.2 us (0.89)
  Pallas kernels: 61.2 us -> 54.2 us
    pallas_call x1, Pallas kernels: 9.08 us -> 4.85 us  [body(): pl.pallas_call(functools.partial(finish_kernel, keep, groups, owners), in...]
    pallas_call x1, Pallas kernels: 52.2 us -> 49.4 us  [body(): pl.pallas_call(functools.partial(sums_kernel, keep, groups, owners), in_s...]
where the time goes in v3:
time: 55.2 us; the launch traced here: 55.1 us
  Pallas kernels  54.2 us (98%)
  between operations  0.82 us (1%)
    pallas_call x1, Pallas kernels, body(): pl.pallas_call(functools.partial(sums_kernel, keep, groups, owners), in_s...  49.4 us
    pallas_call x1, Pallas kernels, body(): pl.pallas_call(functools.partial(finish_kernel, keep, groups, owners), in...  4.85 us

profile of v3, /device:TPU:1, one launch (start us, length us, event | category | flops | bytes accessed | tf_op | source)
XLA Modules:
  0.0 55.1 jit_solution(15190732180921001237)
XLA Ops:
  0.6 0.0 copy-start
  0.6 49.4 %shard_map.68 = (bf16[2048,2048]{1,0:T(8,128)(2,1)S(1)}, f32[7,128,128]{2,1,0:T(8,128)S(1)}, s32[8,384]{1,0:T(8,128)S(1)}) custom-call(s32[1,328]{1,0:T(1,128)} %kept.1, s32[17]{0:T(128)} %bounds.3, bf16[1024,2048]{1,0:T(8,128)(2,1)} %acts_in.1, bf16[1024,2048]{1,0:T(8,128)(2,1)} %grad_in.1, bf16[2048,2048]{1,0:T(8,128)(2,1)} %err_in.1), custom_call_target="tpu_custom_call" | custom-call | tf_op jit(solution)/shard_map/pallas_call | solution.py:376
  50.0 0.0 copy-done
  50.1 4.8 %shard_map.69 = (f32[328,128]{1,0:T(8,128)}, bf16[2048,2048]{1,0:T(8,128)(2,1)}) custom-call(s32[17]{0:T(128)S(1)} %copy-done, s32[8,384]{1,0:T(8,128)S(1)} %get-tuple-element.7.pos, f32[7,128,128]{2,1,0:T(8,128)S(1)} %get-tuple-element.8.back, bf16[2048,2048]{1,0:T(8,128)(2,1)S(1)} %get-tuple-element.9.err_in), custom_call_target="tpu_custom_call" | custom-call | tf_op jit(solution)/shard_map/pallas_call | solution.py:409
Async XLA Ops:
  0.6 49.4 %copy-start = (s32[17]{0:T(128)S(1)}, s32[17]{0:T(128)}, u32[]{:S(2)}) copy-start(s32[17]{0:T(128)} %bounds.3) | copy-start | bytes 208

commit v4 on v3

--- a/solution.py
+++ b/solution.py
@@ -61,7 +61,7 @@
     width = err.shape[1]
     pad = ids_s.shape[1]
     half = n // 2
-    tile = 256
+    tile = 512
     shift = (width // LANES).bit_length() - 1
     per_row = width // LANES
 
@@ -162,24 +162,17 @@
     own = pltpu.make_async_copy(send.at[:, me, :], got.at[:, 0, :], sems.at[6])
     own.start()
 
-    def push(part):
-        def one(o, carry):
-            tg = lax.rem(g + o // owners, groups)
-            td = lax.rem(d + o % owners, owners)
-            pltpu.make_async_remote_copy(
-                src_ref=send.at[:, tg * owners + td, :],
-                dst_ref=got.at[:, o, :],
-                send_sem=sems.at[0],
-                recv_sem=sems.at[1 + part],
-                device_id=(tg, td),
-                device_id_type=MESH,
-            ).start()
-            return carry
-
-        return one
-
-    lax.fori_loop(1, half, push(0), 0)
-    lax.fori_loop(half, n, push(1), 0)
+    def push(o):
+        tg = lax.rem(g + o // owners, groups)
+        td = lax.rem(d + o % owners, owners)
+        pltpu.make_async_remote_copy(
+            src_ref=send.at[:, tg * owners + td, :],
+            dst_ref=got.at[:, o, :],
+            send_sem=sems.at[0],
+            recv_sem=sems.at[1 + o // half],
+            device_id=(tg, td),
+            device_id_type=MESH,
+        ).start()
 
     def product(t, carry):
         rows = pl.ds(pl.multiple_of(t * tile, tile), tile)
@@ -196,6 +189,14 @@
                 ).astype(BF16)
         return carry
 
+    def each(start):
+        def one(o, carry):
+            start(o)
+            return carry
+
+        return one
+
+    lax.fori_loop(1, n, each(push), 0)
     first = width // tile // 2
     lax.fori_loop(0, first, product, 0)
     upper = pl.ds(0, first * tile)
@@ -205,9 +206,9 @@
     total[...] = jnp.zeros(total.shape, F32)
     left = iota((SUB, LANES), 1) < half
     def index_rows(h, p, which):
-        at_p = pl.multiple_of(p * 2 * SUB, 2 * SUB)
+        at_p = p * 2 * SUB
         return jnp.where(
-            left, ct[h, which, pl.ds(at_p, SUB), :], ct[h, which, pl.ds(at_p + SUB, SUB), :]
+            left, ct[h, which, at_p : at_p + SUB, :], ct[h, which, at_p + SUB : at_p + 2 * SUB, :]
         )
 
     def height_of(row):
@@ -222,7 +223,7 @@
         ]
 
     def add(h):
-        def one(p, carry):
+        for p in range(ROWS // 2):
             x = jnp.concatenate(
                 [
                     got[2 * p, h * half : (h + 1) * half, :],
@@ -237,12 +238,9 @@
                 lanes = slice(j * n, (j + 1) * n)
                 oh[step, :, lanes] = height_of(high[j : j + 1, :])
                 hi, lo = put_of(low[j : j + 1, :], x[j * WIDE : (j + 1) * WIDE])
-                put[:LANES, lanes] = hi
-                put[LANES:, lanes] = lo
-            total[...] += dot(oh[step], put[...], 1, 1)
-            return carry
-
-        return one
+                put[step % 2, :LANES, lanes] = hi
+                put[step % 2, LANES:, lanes] = lo
+            total[...] += dot(put[step % 2], oh[step], 1, 1)
 
     own.wait()
     for h in range(2):
@@ -252,7 +250,7 @@
         local = jnp.concatenate([numbers, numbers], axis=0).T.astype(I32) - bounds[2 * g]
         ct[h, 0] = local >> 4
         ct[h, 1] = local & (SUB - 1)
-        lax.fori_loop(0, ROWS // 2, add(h), 0)
+        add(h)
 
     first_half = iota((1, n), 1) < half
     high, low = (
@@ -261,17 +259,17 @@
     )
     oh_last[...] = height_of(high)
     parts = put_of(low, got[ROWS].T[LANES - WIDE :])
-    total[...] += dot(oh_last[...], jnp.concatenate(parts, axis=0), 1, 1)
-
-    whole = total[:, :LANES] + total[:, LANES:]
+    total[...] += dot(jnp.concatenate(parts, axis=0), oh_last[...], 1, 1)
+
+    whole = total[:LANES] + total[LANES:]
     square = whole * whole
-    at_block = iota((heights, LANES), 0) * SUB + iota((heights, LANES), 1) // WIDE
+    at_block = iota((LANES, heights), 1) * SUB + iota((LANES, heights), 0) // WIDE
     in_first = at_block < bounds[2 * g + 1] - bounds[2 * g]
     squares = [
         jnp.sum(jnp.where(in_first, square, 0.0), keepdims=True),
         jnp.sum(jnp.where(in_first, 0.0, square), keepdims=True),
     ]
-    hi, lo = split(whole.T)
+    hi, lo = split(whole)
     table = jnp.concatenate([hi, lo], axis=0)
 
     def pick(both, row):
@@ -288,21 +286,7 @@
         lane < LANES - SUB, jnp.where(lane < LANES // 2, squares[0], squares[1]), last
     )
 
-    def look(h):
-        def one(p, carry):
-            both = dot(table, oh[h * (ROWS // 2) + p], 1, 0)
-            both = both[:LANES] + both[LANES:]
-            low = index_rows(h, p, 1)
-            rows = jnp.concatenate(
-                [pick(both[:, j * n : (j + 1) * n], low[j : j + 1, :]) for j in range(SUB)], axis=0
-            ).T
-            ans[2 * p, h * half : (h + 1) * half, :] = rows[:half]
-            ans[2 * p + 1, h * half : (h + 1) * half, :] = rows[half:]
-            return carry
-
-        return one
-
-    def answer(o, carry):
+    def answer(o):
         tg = lax.rem(g + groups - o // owners, groups)
         td = lax.rem(d + owners - o % owners, owners)
         pltpu.make_async_remote_copy(
@@ -313,15 +297,29 @@
             device_id=(tg, td),
             device_id_type=MESH,
         ).start()
-        return carry
-
-    lax.fori_loop(0, ROWS // 2, look(0), 0)
+
+    def look(h):
+        quad = SUB // 4
+        for p in range(ROWS // 2):
+            low = index_rows(h, p, 1)
+            parts = []
+            for k in range(4):
+                cols = slice(k * quad * n, (k + 1) * quad * n)
+                both = dot(table, oh[h * (ROWS // 2) + p, :, cols], 1, 0)
+                both = both[:LANES] + both[LANES:]
+                for j in range(quad):
+                    row = low[k * quad + j : k * quad + j + 1, :]
+                    parts.append(pick(both[:, j * n : (j + 1) * n], row))
+            rows = jnp.concatenate(parts, axis=0).T
+            ans[2 * p, h * half : (h + 1) * half, :] = rows[:half]
+            ans[2 * p + 1, h * half : (h + 1) * half, :] = rows[half:]
+
+    look(0)
     own = pltpu.make_async_copy(ans.at[:, 0, :], back.at[:, me, :], sems.at[6])
     own.start()
-    lax.fori_loop(1, half, answer, 0)
-    lax.fori_loop(0, ROWS // 2, look(1), 0)
-    lax.fori_loop(half, n, answer, 0)
-
+    lax.fori_loop(1, half, each(answer), 0)
+    look(1)
+    lax.fori_loop(half, n, each(answer), 0)
     lax.fori_loop(first, width // tile, product, 0)
     stores[0].wait()
     lower = pl.ds(first * tile, width - first * tile)
@@ -395,10 +393,10 @@
             pltpu.VMEM((ROWS + 1, n, LANES), F32),
             pltpu.VMEM((ROWS, heights, SUB * n), BF16),
             pltpu.VMEM((heights, n), BF16),
-            pltpu.VMEM((2 * LANES, SUB * n), BF16),
+            pltpu.VMEM((2, 2 * LANES, SUB * n), BF16),
             pltpu.VMEM((ROWS + 1, n, LANES), F32),
             pltpu.VMEM((2, 2, LANES, n), I32),
-            pltpu.VMEM((heights, 2 * LANES), F32),
+            pltpu.VMEM((2 * LANES, heights), F32),
             pltpu.SemaphoreType.DMA((14,)),
             pltpu.SemaphoreType.REGULAR,
         ],

time: 55.2 us -> 53.2 us (0.964)
  Pallas kernels: 54.2 us -> 52.2 us
    pallas_call x1, Pallas kernels: 49.4 us -> 47.4 us  [body(): pl.pallas_call(functools.partial(sums_kernel, keep, groups, owners), in_s...]
where the time goes in v4:
time: 53.2 us; the launch traced here: 53 us
  Pallas kernels  52.2 us (98%)
  between operations  0.84 us (2%)
    pallas_call x1, Pallas kernels, body(): pl.pallas_call(functools.partial(sums_kernel, keep, groups, owners), in_s...  47.4 us
    pallas_call x1, Pallas kernels, body(): pl.pallas_call(functools.partial(finish_kernel, keep, groups, owners), in...  4.85 us

profile of v4, /device:TPU:1, one launch (start us, length us, event | category | flops | bytes accessed | tf_op | source)
XLA Modules:
  0.0 53.0 jit_solution(7011732928797463420)
XLA Ops:
  0.6 0.0 copy-start
  0.6 47.4 %shard_map.68 = (bf16[2048,2048]{1,0:T(8,128)(2,1)S(1)}, f32[7,128,128]{2,1,0:T(8,128)S(1)}, s32[8,384]{1,0:T(8,128)S(1)}) custom-call(s32[1,328]{1,0:T(1,128)} %kept.1, s32[17]{0:T(128)} %bounds.3, bf16[1024,2048]{1,0:T(8,128)(2,1)} %acts_in.1, bf16[1024,2048]{1,0:T(8,128)(2,1)} %grad_in.1, bf16[2048,2048]{1,0:T(8,128)(2,1)} %err_in.1), custom_call_target="tpu_custom_call" | custom-call | tf_op jit(solution)/shard_map/pallas_call | solution.py:374
  48.0 0.0 copy-done
  48.0 4.8 %shard_map.69 = (f32[328,128]{1,0:T(8,128)}, bf16[2048,2048]{1,0:T(8,128)(2,1)}) custom-call(s32[17]{0:T(128)S(1)} %copy-done, s32[8,384]{1,0:T(8,128)S(1)} %get-tuple-element.7.pos, f32[7,128,128]{2,1,0:T(8,128)S(1)} %get-tuple-element.8.back, bf16[2048,2048]{1,0:T(8,128)(2,1)S(1)} %get-tuple-element.9.err_in), custom_call_target="tpu_custom_call" | custom-call | tf_op jit(solution)/shard_map/pallas_call | solution.py:407
Async XLA Ops:
  0.6 47.4 %copy-start = (s32[17]{0:T(128)S(1)}, s32[17]{0:T(128)}, u32[]{:S(2)}) copy-start(s32[17]{0:T(128)} %bounds.3) | copy-start | bytes 208

commit v5 on v4

--- a/solution.py
+++ b/solution.py
@@ -112,7 +112,7 @@
     slot = jnp.sum(jnp.where(of, before, 0.0), axis=0, keepdims=True).astype(I32)
     pos = (region >> 1) * LAST + slot + jnp.where(slot == CAP - 1, SUB - 1, 0)
     pos = jnp.where(live, pos, -1)
-    pos_out[...] = jnp.broadcast_to(pos * owners + region, pos_out.shape)
+    pos_out[...] = pos * owners + region
     at = onehot((iota((LANES, pad), 0) == slot) & live)
     high = jnp.where(of, (ids >> 8).astype(F32), 0.0).astype(BF16)
     low = jnp.where(of, (ids & 255).astype(F32), 0.0).astype(BF16)
@@ -130,14 +130,12 @@
         )
     load_grad.wait()
     kept_rows[...] = dot(sel[...], grad[...], 1, 0)
-    for load, cut in zip(load_err[:-1], cuts):
+    for load in load_err:
         load.wait()
-        kept_rows[...] += dot(rows_of[:, cut], err[cut, :], 1, 0)
-    load_err[-1].wait()
     vals = jnp.zeros((pad, LANES), F32)
     for c in range(0, width, 4 * LANES):
         cols = slice(c, c + 4 * LANES)
-        part = kept_rows[:, cols] + dot(rows_of[:, cuts[-1]], err[cuts[-1], cols], 1, 0)
+        part = kept_rows[:, cols] + dot(rows_of[...], err[:, cols], 1, 0)
         for b in range(4):
             vals = jnp.where(
                 kappa == c // LANES + b, part[:, b * LANES : (b + 1) * LANES], vals
@@ -378,7 +376,7 @@
         out_shape=[
             pltpu.VMEM((width, width), BF16),
             pltpu.VMEM((ROWS + 1, n, LANES), F32),
-            pltpu.VMEM((8, pad), I32),
+            pltpu.VMEM((1, pad), I32),
         ],
         scratch_shapes=[
             pltpu.VMEM((tokens, width), BF16),

time: 53.2 us -> 52.6 us (0.989)
  Pallas kernels: 52.2 us -> 51.6 us
where the time goes in v5:
time: 52.6 us; the launch traced here: 52.5 us
  Pallas kernels  51.6 us (98%)
  between operations  0.84 us (2%)
    pallas_call x1, Pallas kernels, body(): pl.pallas_call(functools.partial(sums_kernel, keep, groups, owners), in_s...  47 us
    pallas_call x1, Pallas kernels, body(): pl.pallas_call(functools.partial(finish_kernel, keep, groups, owners), in...  4.67 us

profile of v5, /device:TPU:1, one launch (start us, length us, event | category | flops | bytes accessed | tf_op | source)
XLA Modules:
  0.0 52.5 jit_solution(3510651289778906950)
XLA Ops:
  0.6 0.0 copy-start
  0.6 47.0 %shard_map.68 = (bf16[2048,2048]{1,0:T(8,128)(2,1)S(1)}, f32[7,128,128]{2,1,0:T(8,128)S(1)}, s32[1,384]{1,0:T(1,128)S(1)}) custom-call(s32[1,328]{1,0:T(1,128)} %kept.1, s32[17]{0:T(128)} %bounds.3, bf16[1024,2048]{1,0:T(8,128)(2,1)} %acts_in.1, bf16[1024,2048]{1,0:T(8,128)(2,1)} %grad_in.1, bf16[2048,2048]{1,0:T(8,128)(2,1)} %err_in.1), custom_call_target="tpu_custom_call" | custom-call | tf_op jit(solution)/shard_map/pallas_call | solution.py:372
  47.6 0.0 copy-done
  47.6 4.7 %shard_map.69 = (f32[328,128]{1,0:T(8,128)}, bf16[2048,2048]{1,0:T(8,128)(2,1)}) custom-call(s32[17]{0:T(128)S(1)} %copy-done, s32[1,384]{1,0:T(1,128)S(1)} %get-tuple-element.7.pos, f32[7,128,128]{2,1,0:T(8,128)S(1)} %get-tuple-element.8.back, bf16[2048,2048]{1,0:T(8,128)(2,1)S(1)} %get-tuple-element.9.err_in), custom_call_target="tpu_custom_call" | custom-call | tf_op jit(solution)/shard_map/pallas_call | solution.py:405
Async XLA Ops:
  0.6 47.0 %copy-start = (s32[17]{0:T(128)S(1)}, s32[17]{0:T(128)}, u32[]{:S(2)}) copy-start(s32[17]{0:T(128)} %bounds.3) | copy-start | bytes 208
